TPU v7x, 32 devices: a whole 2x2x4 slice. The times are simulated.
32 devices in a mesh: gz: 8 (over y, x, core), gy: 4 (over z).
Axes of the slice: x: 2, y: 2, z: 4, core: 2. Of those that a mesh axis runs over, the one named last changes fastest.
Arguments:
- coarse_six: float32 [64, 1024, 512], P('gz', 'gy'), may hold values from 0.1 to 10
Outputs:
- detail_seven: float32 [64, 1024, 512], P('gz', 'gy')
- coarse_seven: float32 [64, 1024, 512], P('gz', 'gy')
All inputs are finite; a program needn't handle non-finite values.
Results may differ from a plain program's by a relative error of at most 0.00002.
Values sent between devices are 32-bit elements; how exact they have to be, the bound alone decides.
No kernel may reach another device: no remote copies, remote signals or barrier semaphores. Data moves between devices by JAX's collectives and lax.ppermute only.
A program may use at most 128 MiB of HBM per device.

v0:
```python
import functools
import math

import jax
import jax.numpy as jnp
from jax import lax
from jax.experimental import pallas as pl
from jax.experimental.pallas import tpu as pltpu
from jax.sharding import PartitionSpec as P

TAP_DILATION = 32
REACH = 2 * TAP_DILATION
LANES = 128
STRIP = 8
UNIT_ROWS = 128
FIRST_PLANES = 3
LATER_GROUPS = (((2, 1),), ((2, 1), (1, 2)))

kernel_weights = (0.0625, 0.25, 0.375, 0.25, 0.0625)


def passed_along(x, axis, by):
    peers = lax.axis_size(axis)
    return lax.ppermute(x, axis, [(i, (i + by) % peers) for i in range(peers)])


def z_taps(plane_stack, count):
    weights = {}
    for cell_position in range(5):
        filter_reach = (cell_position - 2) * TAP_DILATION // plane_stack
        moved = -filter_reach % count
        weights[moved] = weights.get(moved, 0.0) + kernel_weights[cell_position]
    own = weights.pop(0, 0.0)
    return own, weights


def lane_of(shape):
    return lax.broadcasted_iota(jnp.int32, shape, 1)


def x_taps():
    return {(cell_position - 2) * TAP_DILATION: kernel_weights[cell_position] for cell_position in range(5)}


def rest_taps():
    return {(cell_position - 2) * TAP_DILATION: weight for cell_position, weight in enumerate((0.125, 0.375, 0.375, 0.125))}


def pair_sums(rows):
    return (rows + pltpu.roll(rows, rows.shape[1] - TAP_DILATION, 1)) * 0.5


def fill_matrix(matrix_ref, taps):
    depth, width = matrix_ref.shape
    for start in range(0, depth, LANES):
        shape = (LANES, width)
        row = start + lax.broadcasted_iota(jnp.int32, shape, 0)
        offset = row - lax.broadcasted_iota(jnp.int32, shape, 1)
        offset = jnp.where(offset < 0, offset + width, offset)
        values = jnp.zeros(shape, jnp.float32)
        for tap, weight in taps.items():
            values = jnp.where(offset == tap % width, weight, values)
        matrix_ref[pl.ds(start, LANES), :] = values.astype(jnp.bfloat16)


def x_smoothed(rows, matrix):
    parts = []
    for _ in range(3):
        parts.append(rows.astype(jnp.bfloat16))
        rows = rows - parts[-1].astype(jnp.float32)
    terms = jnp.dot(jnp.concatenate(parts), matrix, preferred_element_type=jnp.float32)
    high, middle, low = jnp.split(terms, 3)
    return high + middle + low


def y_sums(groups):
    for _ in range(4):
        groups = [a + b for a, b in zip(groups[:-1], groups[1:])]
    return groups


def packed_rows(width):
    return UNIT_ROWS - UNIT_ROWS * TAP_DILATION // width


def store_packed(out_ref, place, smooth):
    rows, width = smooth.shape
    kept_rows = out_ref.shape[1]
    depth = rows - kept_rows
    out_ref[place, :, : width - LANES] = smooth[:kept_rows, : width - LANES]
    kept = lane_of((depth, LANES)) < LANES - TAP_DILATION
    for piece in range(kept_rows // depth):
        tile = piece * TAP_DILATION // LANES
        shift = (LANES - TAP_DILATION - piece * TAP_DILATION) % LANES
        moved = smooth[kept_rows:, tile * LANES : (tile + 1) * LANES]
        if shift:
            moved = pltpu.roll(moved, shift, 1)
        last = smooth[piece * depth : (piece + 1) * depth, width - LANES :]
        out_ref[place, pl.ds(piece * depth, depth), width - LANES :] = jnp.where(kept, last, moved)


def completed(strip):
    width = strip.shape[1]
    last = strip[:, width - LANES :]
    lane = lane_of(last.shape)
    kept = lane < LANES - TAP_DILATION
    total = jnp.where(kept, last, 0.0)
    for start in range(0, width - LANES, LANES):
        total = total + strip[:, start : start + LANES]
    odd = (lane // TAP_DILATION) % 2 == 1
    total = jnp.where(odd, -total, total)
    total = total + pltpu.roll(total, 2 * TAP_DILATION, 1)
    total = total + pltpu.roll(total, TAP_DILATION, 1)
    return jnp.concatenate([strip[:, : width - LANES], jnp.where(kept, last, total)], axis=1)


def unpacked(weights, refs, use):
    kept_rows, width = refs[0].shape[1:]
    depth = UNIT_ROWS - kept_rows
    tiles = [None] * (width // LANES)
    for piece in range(kept_rows // depth):
        rows = pl.ds(piece * depth, depth)
        strip = weighted(weights, [ref[0, rows, :] for ref in refs])
        tile = piece * TAP_DILATION // LANES
        shift = (piece * TAP_DILATION - (LANES - TAP_DILATION)) % LANES
        moved = strip[:, width - LANES :]
        if shift:
            moved = pltpu.roll(moved, shift, 1)
        if tiles[tile] is None:
            tiles[tile] = moved
        else:
            here = lane_of(moved.shape) // TAP_DILATION == piece % (LANES // TAP_DILATION)
            tiles[tile] = jnp.where(here, moved, tiles[tile])
        use(rows, completed(strip))
    use(pl.ds(kept_rows, depth), completed(jnp.concatenate(tiles, axis=1)))


def weighted(weights, values):
    total = None
    for weight, value in zip(weights, values):
        term = weight * value
        total = term if total is None else total + term
    return total


def pair_kernel(units_ref, out_ref, read_ref, read_sem):
    read = pltpu.make_async_copy(units_ref.at[0], read_ref, read_sem)
    read.start()
    read.wait()
    store_packed(out_ref, 0, pair_sums(read_ref[...]))


def x_kernel(first, units_ref, out_ref, read_ref, matrix_ref, read_sems):
    count = out_ref.shape[0]

    def read(unit):
        return pltpu.make_async_copy(units_ref.at[first + unit], read_ref.at[unit], read_sems.at[unit])

    for unit in range(count):
        read(unit).start()
    fill_matrix(matrix_ref, x_taps())

    @pl.loop(0, count)
    def _(unit):
        read(unit).wait()
        store_packed(out_ref, unit, x_smoothed(read_ref[unit], matrix_ref[...]))


def extended_groups(before_ref, c_ref, after_ref, offset):
    groups = []
    for ref in (before_ref, c_ref, after_ref):
        for start in range(0, ref.shape[1], TAP_DILATION):
            groups.append(ref[0, pl.ds(start + offset, STRIP), :])
    return groups


def yx_kernel(before_ref, c_ref, after_ref, *refs):
    *out_refs, matrix_ref, smooth_ref = refs
    pl.when(pl.program_id(0) == 0)(lambda: fill_matrix(matrix_ref, x_taps()))
    for within in range(TAP_DILATION // STRIP):
        groups = y_sums(extended_groups(before_ref, c_ref, after_ref, within * STRIP))
        for group, strip in enumerate(groups):
            smooth_ref[pl.ds(group * TAP_DILATION + within * STRIP, STRIP), :] = strip * (1.0 / 16.0)
    places = [(ref, place) for ref in out_refs for place in range(ref.shape[0])]
    for unit, (ref, place) in enumerate(places):
        smooth = x_smoothed(smooth_ref[pl.ds(unit * UNIT_ROWS, UNIT_ROWS), :], matrix_ref[...])
        store_packed(ref, place, smooth)


def z_kernel(weights, *refs):
    whole_ref = refs[-1]

    def use(rows, strip):
        whole_ref[0, rows, :] = strip

    unpacked(weights, refs[: len(weights)], use)


def pair_z_kernel(weights, *refs):
    whole_ref, matrix_ref, pair_ref = refs[-3:]
    fill_matrix(matrix_ref, rest_taps())

    def use(rows, strip):
        pair_ref[rows, :] = strip

    unpacked(weights, refs[: len(weights)], use)
    whole_ref[0] = x_smoothed(pair_ref[...], matrix_ref[...])


def y_kernel(before_ref, whole_ref, after_ref, c_ref, detail_ref, coarse_ref):
    scale = 1.0 / 16.0
    for within in range(TAP_DILATION // STRIP):
        groups = y_sums(extended_groups(before_ref, whole_ref, after_ref, within * STRIP))
        for group, strip in enumerate(groups):
            rows = pl.ds(group * TAP_DILATION + within * STRIP, STRIP)
            coarse = strip * scale
            coarse_ref[0, rows, :] = coarse
            detail_ref[0, rows, :] = c_ref[0, rows, :] - coarse


def finish_kernel(weights, *refs):
    c_ref, _, _, detail_ref, coarse_ref = refs[len(weights) :]

    def use(rows, strip):
        coarse_ref[0, rows, :] = strip
        detail_ref[0, rows, :] = c_ref[0, rows, :] - strip

    unpacked(weights, refs[: len(weights)], use)


def last_kernel(weights, place, *refs):
    units_ref, _, _, detail_ref, coarse_ref, results_ref, write_sems = refs[len(weights) :]
    half = UNIT_ROWS // 2

    def write(piece, output, ref):
        rows = pl.ds(piece * half, half)
        source = results_ref.at[output, rows]
        return pltpu.make_async_copy(source, ref.at[place, rows], write_sems.at[piece, output])

    writes = [[write(piece, 0, detail_ref), write(piece, 1, coarse_ref)] for piece in range(2)]

    def use(rows, strip):
        results_ref[1, rows, :] = strip
        results_ref[0, rows, :] = units_ref[place, rows, :] - strip
        piece, left = divmod(rows.start + rows.size, half)
        if left == 0:
            for copy in writes[piece - 1]:
                copy.start()

    unpacked(weights, refs[: len(weights)], use)
    for copies in writes:
        for copy in copies:
            copy.wait()


def block_of(rows, width, first=0, depth=1):
    return pl.BlockSpec((depth, rows, width), lambda step: (first + step, 0, 0))


def anywhere():
    return pl.BlockSpec(memory_space=pl.ANY)


def in_vmem():
    return pl.BlockSpec(memory_space=pltpu.VMEM)


def call(kernel, name, steps, in_specs, out_specs, out_shape, args, aliases=None, scratch=(), grant=24):
    blocks = [spec.block_shape for spec in (*in_specs, *out_specs) if spec.block_shape]
    moved = 4 * max(steps, 1) * sum(math.prod(block) for block in blocks)
    return pl.pallas_call(
        kernel,
        grid=(steps,) if steps else (),
        in_specs=in_specs,
        out_specs=out_specs,
        out_shape=out_shape,
        scratch_shapes=scratch,
        input_output_aliases=aliases or {},
        compiler_params=pltpu.CompilerParams(vmem_limit_bytes=grant * 1024 * 1024),
        cost_estimate=pl.CostEstimate(flops=moved * 2, bytes_accessed=moved, transcendentals=0),
        name=name,
    )(*args)


def in_hbm(x):
    return pltpu.with_memory_space_constraint(x, pltpu.HBM)


def f32(*shape):
    return jax.ShapeDtypeStruct(shape, jnp.float32)


def shards(coarse_six):
    planes, rows, width = coarse_six.shape
    short = packed_rows(width)
    own, shifts = z_taps(planes, lax.axis_size("gz"))
    weights = (own, *shifts.values())
    count = len(weights)
    whole, unit, packed, edge = (functools.partial(block_of, n, width) for n in (rows, UNIT_ROWS, short, REACH))
    parts = rows // UNIT_ROWS
    units = coarse_six.reshape(planes * parts, UNIT_ROWS, width)
    matrix = pltpu.VMEM((width, width), jnp.bfloat16)

    def along_gz(x):
        return [passed_along(x, "gz", moved) for moved in shifts]

    def halo(source, start, stop):
        top, bottom = source[start:stop, :REACH], source[start:stop, rows - REACH :]
        return passed_along(bottom, "gy", 1), passed_along(top, "gy", -1)

    sums_shape = f32(FIRST_PLANES * parts, UNIT_ROWS, width)
    lead = call(
        pair_kernel,
        "pair_x",
        0,
        [anywhere()],
        [in_vmem()],
        [pltpu.VMEM((1, short, width), jnp.float32)],
        [in_hbm(units)],
        scratch=[pltpu.VMEM((UNIT_ROWS, width), jnp.float32), pltpu.SemaphoreType.DMA(())],
    )[0]
    lead, ready = lax.optimization_barrier((lead, units))
    lead_moved = along_gz(lead)
    first = FIRST_PLANES * parts - 1
    first_block = call(
        functools.partial(x_kernel, 1),
        "smooth_x",
        0,
        [anywhere()],
        [in_vmem()],
        [pltpu.VMEM((first, short, width), jnp.float32)],
        [in_hbm(ready)],
        scratch=[
            pltpu.VMEM((first, UNIT_ROWS, width), jnp.float32),
            matrix,
            pltpu.SemaphoreType.DMA((first,)),
        ],
    )[0]
    first_block, ready = lax.optimization_barrier((first_block, ready))
    first_moved = along_gz(first_block)
    sums = call(
        functools.partial(pair_z_kernel, weights),
        "smooth_zx",
        1,
        [packed()] * count,
        [unit()],
        [sums_shape],
        [lead, *lead_moved],
        scratch=[matrix, pltpu.VMEM((UNIT_ROWS, width), jnp.float32)],
    )

    later = []
    start = FIRST_PLANES
    sums, ready = lax.optimization_barrier((sums, coarse_six))
    near = halo(ready, start, start + sum(size for size, _ in LATER_GROUPS[0]))
    for number, sizes in enumerate(LATER_GROUPS):
        offset = 0
        for size, messages in sizes:
            depth = parts // messages
            blocks = call(
                yx_kernel,
                "smooth_yx",
                size,
                [edge(offset), whole(start + offset), edge(offset)],
                [packed(depth=depth)] * messages,
                [f32(size * depth, short, width)] * messages,
                [near[0], in_hbm(coarse_six), near[1]],
                scratch=[matrix, pltpu.VMEM((rows, width), jnp.float32)],
            )
            for message, block in enumerate(blocks):
                place = (start + offset) * parts + message * depth
                later.append((place, size * depth, (block, *along_gz(block))))
            offset += size
        start += offset
        if number == 0:
            block, ready = lax.optimization_barrier((block, ready))
            block, *first_moved = lax.optimization_barrier((block, *first_moved))
            sums = call(
                functools.partial(z_kernel, weights),
                "smooth_z",
                first,
                [packed()] * count + [anywhere()],
                [unit(1)],
                [sums_shape],
                [first_block, *first_moved, *sums],
                {count: 0},
            )[0]
            along_z = sums.reshape(FIRST_PLANES, rows, width)
            sides = halo(along_z, 0, FIRST_PLANES)
        if number + 1 < len(LATER_GROUPS):
            near = halo(ready, start, start + sum(size for size, _ in LATER_GROUPS[number + 1]))
            near, along_z = lax.optimization_barrier((near, along_z))

    block, sides = lax.optimization_barrier((block, sides))
    outs = call(
        y_kernel,
        "smooth_y",
        FIRST_PLANES,
        [edge(), whole(), edge(), whole()],
        [whole(), whole()],
        [f32(planes, rows, width)] * 2,
        [sides[0], along_z, sides[1], coarse_six],
    )
    outs = [out.reshape(units.shape) for out in outs]
    for place, size, blocks in later[:-1]:
        outs, blocks = lax.optimization_barrier((outs, blocks))
        outs = call(
            functools.partial(finish_kernel, weights),
            "finish",
            size,
            [packed()] * count + [unit(place)] + [anywhere()] * 2,
            [unit(place)] * 2,
            [f32(*units.shape)] * 2,
            [*blocks, units, *outs],
            {count + 1: 0, count + 2: 1},
        )
    place, _, blocks = later[-1]
    outs, blocks = lax.optimization_barrier((outs, blocks))
    outs = call(
        functools.partial(last_kernel, weights, place),
        "finish_last",
        0,
        [in_vmem()] * (count + 1) + [anywhere()] * 2,
        [anywhere()] * 2,
        [f32(*units.shape)] * 2,
        [*blocks, units, *outs],
        {count + 1: 0, count + 2: 1},
        scratch=[
            pltpu.VMEM((2, UNIT_ROWS, width), jnp.float32),
            pltpu.SemaphoreType.DMA((2, 2)),
        ],
    )
    return tuple(out.reshape(coarse_six.shape) for out in outs)


def solution(mesh):
    return jax.shard_map(
        shards,
        mesh=mesh,
        in_specs=(P("gz", "gy", None),),
        out_specs=(P("gz", "gy", None), P("gz", "gy", None)),
        check_vma=False,
    )
```

profile of v0, /device:TPU:0, one launch (start us, length us, event | category | flops | bytes accessed | tf_op | source)
XLA Modules:
  0.0 90.7 jit_solution(16140873523478462869)
XLA Ops:
  0.6 1.1 %pair_x.1.refs_0_ = f32[1,120,512]{2,1,0:T(8,128)S(1)} custom-call(f32[16,128,512]{2,1,0:T(8,128)} %bitcast.6), custom_call_target="tpu_custom_call" | custom-call | tf_op jit(solution)/shard_map/pair_x/pallas_call | solution.py:271
  1.8 3.0 %collective-permute-start = (f32[1,120,512]{2,1,0:T(8,128)S(1)}, f32[1,120,512]{2,1,0:T(8,128)S(1)}, u32[]{:S(2)}, u32[]{:S(2)}) collective-permute-start(f32[1,120,512]{2,1,0:T(8,128)S(1)} %pair_x.1.refs_0_), channel_id=1, source_target_pairs={{0,16},{4,20},{8,24},{12,28},{16,0},{20,4},{24,8},{28,12},{1,17},{... | collective-permute-start | bytes 737288 | tf_op jit(solution)/shard_map/ppermute | solution.py:24
  4.8 3.3 %smooth_x.1.refs_0_ = f32[5,120,512]{2,1,0:T(8,128)S(1)} custom-call(f32[16,128,512]{2,1,0:T(8,128)} %bitcast.7), custom_call_target="tpu_custom_call" | custom-call | tf_op jit(solution)/shard_map/smooth_x/pallas_call | solution.py:271
  8.1 0.1 collective-permute-start.5
  8.2 3.0 %collective-permute-done.refs_1_ = f32[1,120,512]{2,1,0:T(8,128)S(1)} collective-permute-done((f32[1,120,512]{2,1,0:T(8,128)S(1)}, f32[1,120,512]{2,1,0:T(8,128)S(1)}, u32[]{:S(2)}, u32[]{:S(2)}) %collective-permute-start) | collective-permute-done | bytes 245792 | tf_op jit(solution)/shard_map/ppermute | solution.py:24
  11.1 0.6 smooth_zx.1.refs_2_
  11.7 1.1 %fusion.1 = (f32[2,64,512]{2,1,0:T(8,128)S(1)}, f32[2,64,512]{2,1,0:T(8,128)S(1)}) fusion(f32[8,256,512]{2,1,0:T(8,128)} %c_ref.7), kind=kLoop, calls=%fused_computation.1 | loop fusion | bytes 1048576 | tf_op jit(solution)/shard_map/slice | solution.py:308
  12.8 2.1 %collective-permute-start.1 = (f32[2,64,512]{2,1,0:T(8,128)S(1)}, f32[2,64,512]{2,1,0:T(8,128)S(1)}, u32[]{:S(2)}, u32[]{:S(2)}) collective-permute-start(f32[2,64,512]{2,1,0:T(8,128)S(1)} %get-tuple-element.83), channel_id=1, source_target_pairs={{0,1},{1,2},{2,3},{3,0},{4,5},{5,6},{6,7},{7,4},{8,9},{9,10},{10,1... | collective-permute-start | bytes 786440 | tf_op jit(solution)/shard_map/ppermute | solution.py:24
  14.9 2.1 %collective-permute-start.2 = (f32[2,64,512]{2,1,0:T(8,128)S(1)}, f32[2,64,512]{2,1,0:T(8,128)S(1)}, u32[]{:S(2)}, u32[]{:S(2)}) collective-permute-start(f32[2,64,512]{2,1,0:T(8,128)S(1)} %get-tuple-element.82), channel_id=1, source_target_pairs={{0,3},{1,0},{2,1},{3,2},{4,7},{5,4},{6,5},{7,6},{8,11},{9,8},{10,9... | collective-permute-start | bytes 786440 | tf_op jit(solution)/shard_map/ppermute | solution.py:24
  16.9 7.2 %collective-permute-done.1.before_ref = f32[2,64,512]{2,1,0:T(8,128)S(1)} collective-permute-done((f32[2,64,512]{2,1,0:T(8,128)S(1)}, f32[2,64,512]{2,1,0:T(8,128)S(1)}, u32[]{:S(2)}, u32[]{:S(2)}) %collective-permute-start.1) | collective-permute-done | bytes 262176 | tf_op jit(solution)/shard_map/ppermute | solution.py:24
  24.1 2.6 %collective-permute-done.2.after_ref = f32[2,64,512]{2,1,0:T(8,128)S(1)} collective-permute-done((f32[2,64,512]{2,1,0:T(8,128)S(1)}, f32[2,64,512]{2,1,0:T(8,128)S(1)}, u32[]{:S(2)}, u32[]{:S(2)}) %collective-permute-start.2) | collective-permute-done | bytes 262176 | tf_op jit(solution)/shard_map/ppermute | solution.py:24
  26.7 2.6 %smooth_yx.3.refs_0_ = f32[4,120,512]{2,1,0:T(8,128)S(1)} custom-call(f32[2,64,512]{2,1,0:T(8,128)S(1)} %collective-permute-done.1.before_ref, f32[8,256,512]{2,1,0:T(8,128)} %c_ref.7, f32[2,64,512]{2,1,0:T(8,128)S(1)} %collective-permute-done.2.after_ref), custom_call_target="tpu_custom_call" | custom-call | flops 5111808 | bytes 2555904 | tf_op jit(solution)/shard_map/smooth_yx/pallas_call | solution.py:271
  29.3 1.2 %fusion = (f32[3,64,512]{2,1,0:T(8,128)S(1)}, f32[3,64,512]{2,1,0:T(8,128)S(1)}) fusion(f32[8,256,512]{2,1,0:T(8,128)} %c_ref.7), kind=kLoop, calls=%fused_computation | loop fusion | bytes 1572864 | tf_op jit(solution)/shard_map/slice | solution.py:308
  30.5 1.2 %collective-permute-start.3 = (f32[3,64,512]{2,1,0:T(8,128)S(1)}, f32[3,64,512]{2,1,0:T(8,128)S(1)}, u32[]{:S(2)}, u32[]{:S(2)}) collective-permute-start(f32[3,64,512]{2,1,0:T(8,128)S(1)} %get-tuple-element.81), channel_id=1, source_target_pairs={{0,1},{1,2},{2,3},{3,0},{4,5},{5,6},{6,7},{7,4},{8,9},{9,10},{10,1... | collective-permute-start | bytes 1179656 | tf_op jit(solution)/shard_map/ppermute | solution.py:24
  31.8 2.7 %collective-permute-start.4 = (f32[3,64,512]{2,1,0:T(8,128)S(1)}, f32[3,64,512]{2,1,0:T(8,128)S(1)}, u32[]{:S(2)}, u32[]{:S(2)}) collective-permute-start(f32[3,64,512]{2,1,0:T(8,128)S(1)} %get-tuple-element.80), channel_id=1, source_target_pairs={{0,3},{1,0},{2,1},{3,2},{4,7},{5,4},{6,5},{7,6},{8,11},{9,8},{10,9... | collective-permute-start | bytes 1179656 | tf_op jit(solution)/shard_map/ppermute | solution.py:24
  34.4 1.5 %collective-permute-start.8 = (f32[4,120,512]{2,1,0:T(8,128)S(1)}, f32[4,120,512]{2,1,0:T(8,128)S(1)}, u32[]{:S(2)}, u32[]{:S(2)}) collective-permute-start(f32[4,120,512]{2,1,0:T(8,128)S(1)} %smooth_yx.3.refs_0_), channel_id=1, source_target_pairs={{0,16},{4,20},{8,24},{12,28},{16,0},{20,4},{24,8},{28,12},{1,17},{... | collective-permute-start | bytes 2949128 | tf_op jit(solution)/shard_map/ppermute | solution.py:24
  35.9 2.2 %collective-permute-done.5.refs_1_ = f32[5,120,512]{2,1,0:T(8,128)S(1)} collective-permute-done((f32[5,120,512]{2,1,0:T(8,128)S(1)}, f32[5,120,512]{2,1,0:T(8,128)S(1)}, u32[]{:S(2)}, u32[]{:S(2)}) %collective-permute-start.5) | collective-permute-done | bytes 1228832 | tf_op jit(solution)/shard_map/ppermute | solution.py:24
  38.1 1.1 %smooth_z.1 = f32[6,128,512]{2,1,0:T(8,128)S(1)} custom-call(f32[5,120,512]{2,1,0:T(8,128)S(1)} %smooth_x.1.refs_0_, f32[5,120,512]{2,1,0:T(8,128)S(1)} %collective-permute-done.5.refs_1_, f32[6,128,512]{2,1,0:T(8,128)S(1)} %smooth_zx.1.refs_2_), custom_call_target="tpu_custom_call", output_to_operand_aliasing={{}: (2, {})} | custom-call | flops 7536640 | bytes 3768320 | tf_op jit(solution)/shard_map/smooth_z/pallas_call | solution.py:271
  39.3 5.2 %collective-permute-done.3.before_ref = f32[3,64,512]{2,1,0:T(8,128)S(1)} collective-permute-done((f32[3,64,512]{2,1,0:T(8,128)S(1)}, f32[3,64,512]{2,1,0:T(8,128)S(1)}, u32[]{:S(2)}, u32[]{:S(2)}) %collective-permute-start.3) | collective-permute-done | bytes 393248 | tf_op jit(solution)/shard_map/ppermute | solution.py:24
  44.5 6.5 %collective-permute-done.4.after_ref = f32[3,64,512]{2,1,0:T(8,128)S(1)} collective-permute-done((f32[3,64,512]{2,1,0:T(8,128)S(1)}, f32[3,64,512]{2,1,0:T(8,128)S(1)}, u32[]{:S(2)}, u32[]{:S(2)}) %collective-permute-start.4) | collective-permute-done | bytes 393248 | tf_op jit(solution)/shard_map/ppermute | solution.py:24
  50.9 2.6 %smooth_yx.5.refs_0_ = f32[4,120,512]{2,1,0:T(8,128)S(1)} custom-call(f32[3,64,512]{2,1,0:T(8,128)S(1)} %collective-permute-done.3.before_ref, f32[8,256,512]{2,1,0:T(8,128)} %c_ref.7, f32[3,64,512]{2,1,0:T(8,128)S(1)} %collective-permute-done.4.after_ref), custom_call_target="tpu_custom_call" | custom-call | flops 5111808 | bytes 2555904 | tf_op jit(solution)/shard_map/smooth_yx/pallas_call | solution.py:271
  53.5 0.0 copy-start
  53.5 0.9 collective-permute-start.9
  54.4 0.1 fusion.2
  54.5 0.4 collective-permute-start.6
  54.9 3.5 %collective-permute-start.7 = (f32[3,64,512]{2,1,0:T(8,128)S(1)}, f32[3,64,512]{2,1,0:T(8,128)S(1)}, u32[]{:S(2)}, u32[]{:S(2)}) collective-permute-start(f32[3,64,512]{2,1,0:T(8,128)S(1)} %get-tuple-element.84), channel_id=1, source_target_pairs={{0,3},{1,0},{2,1},{3,2},{4,7},{5,4},{6,5},{7,6},{8,11},{9,8},{10,9... | collective-permute-start | bytes 1179656 | tf_op jit(solution)/shard_map/ppermute | solution.py:24
  58.4 1.9 %smooth_yx.4 = (f32[1,120,512]{2,1,0:T(8,128)S(1)}, f32[1,120,512]{2,1,0:T(8,128)S(1)}) custom-call(f32[3,64,512]{2,1,0:T(8,128)S(1)} %collective-permute-done.3.before_ref, f32[8,256,512]{2,1,0:T(8,128)} %c_ref.7, f32[3,64,512]{2,1,0:T(8,128)S(1)} %collective-permute-done.4.after_ref), custom_call_target="tpu_custom_call" | custom-call | flops 2555904 | bytes 1277952 | tf_op jit(solution)/shard_map/smooth_yx/pallas_call | solution.py:271
  60.3 1.3 %collective-permute-start.10 = (f32[1,120,512]{2,1,0:T(8,128)S(1)}, f32[1,120,512]{2,1,0:T(8,128)S(1)}, u32[]{:S(2)}, u32[]{:S(2)}) collective-permute-start(f32[1,120,512]{2,1,0:T(8,128)S(1)} %get-tuple-element.68.refs_0_), channel_id=1, source_target_pairs={{0,16},{4,20},{8,24},{12,28},{16,0},{20,4},{24,8},{28,12},{1,17},{... | collective-permute-start | bytes 737288 | tf_op jit(solution)/shard_map/ppermute | solution.py:24
  61.6 6.8 %collective-permute-done.6.before_ref = f32[3,64,512]{2,1,0:T(8,128)S(1)} collective-permute-done((f32[3,64,512]{2,1,0:T(8,128)S(1)}, f32[3,64,512]{2,1,0:T(8,128)S(1)}, u32[]{:S(2)}, u32[]{:S(2)}) %collective-permute-start.6) | collective-permute-done | bytes 393248 | tf_op jit(solution)/shard_map/ppermute | solution.py:24
  68.4 1.2 %collective-permute-start.11 = (f32[1,120,512]{2,1,0:T(8,128)S(1)}, f32[1,120,512]{2,1,0:T(8,128)S(1)}, u32[]{:S(2)}, u32[]{:S(2)}) collective-permute-start(f32[1,120,512]{2,1,0:T(8,128)S(1)} %get-tuple-element.74.refs_0_), channel_id=1, source_target_pairs={{0,16},{4,20},{8,24},{12,28},{16,0},{20,4},{24,8},{28,12},{1,17},{... | collective-permute-start | bytes 737288 | tf_op jit(solution)/shard_map/ppermute | solution.py:24
  69.6 3.4 %collective-permute-done.7.after_ref = f32[3,64,512]{2,1,0:T(8,128)S(1)} collective-permute-done((f32[3,64,512]{2,1,0:T(8,128)S(1)}, f32[3,64,512]{2,1,0:T(8,128)S(1)}, u32[]{:S(2)}, u32[]{:S(2)}) %collective-permute-start.7) | collective-permute-done | bytes 393248 | tf_op jit(solution)/shard_map/ppermute | solution.py:24
  73.0 0.0 copy-done
  73.0 2.2 %smooth_y.1 = (f32[8,256,512]{2,1,0:T(8,128)}, f32[8,256,512]{2,1,0:T(8,128)}) custom-call(f32[3,64,512]{2,1,0:T(8,128)S(1)} %collective-permute-done.6.before_ref, f32[3,256,512]{2,1,0:T(8,128)S(1)} %bitcast.13, f32[3,64,512]{2,1,0:T(8,128)S(1)} %collective-permute-done.7.after_ref, f32[8,256,512]{2,1,0:T(8,128)S(1)} %copy-done), custom_call_target="tpu_custom_call" | custom-call | flops 14155776 | bytes 7077888 | tf_op jit(solution)/shard_map/smooth_y/pallas_call | solution.py:271
  75.2 0.0 collective-permute-done.8.refs_1_
  75.2 2.3 %finish.3 = (f32[16,128,512]{2,1,0:T(8,128)}, f32[16,128,512]{2,1,0:T(8,128)}) custom-call(f32[4,120,512]{2,1,0:T(8,128)S(1)} %smooth_yx.3.refs_0_, f32[4,120,512]{2,1,0:T(8,128)S(1)} %collective-permute-done.8.refs_1_, f32[16,128,512]{2,1,0:T(8,128)S(1)} %bitcast.8, f32[16,128,512]{2,1,0:T(8,128)} %bitcast.14, ...), custom_call_target="tpu_custom_call", output_to_operand_aliasing={{0}: (3, {}), {1}: (4, {})} | custom-call | flops 10223616 | bytes 5111808 | tf_op jit(solution)/shard_map/finish/pallas_call | solution.py:271
  77.5 2.7 %collective-permute-done.9.refs_1_ = f32[4,120,512]{2,1,0:T(8,128)S(1)} collective-permute-done((f32[4,120,512]{2,1,0:T(8,128)S(1)}, f32[4,120,512]{2,1,0:T(8,128)S(1)}, u32[]{:S(2)}, u32[]{:S(2)}) %collective-permute-start.9) | collective-permute-done | bytes 983072 | tf_op jit(solution)/shard_map/ppermute | solution.py:24
  80.2 2.3 %finish.4 = (f32[16,128,512]{2,1,0:T(8,128)}, f32[16,128,512]{2,1,0:T(8,128)}) custom-call(f32[4,120,512]{2,1,0:T(8,128)S(1)} %smooth_yx.5.refs_0_, f32[4,120,512]{2,1,0:T(8,128)S(1)} %collective-permute-done.9.refs_1_, f32[16,128,512]{2,1,0:T(8,128)S(1)} %bitcast.9, ...), custom_call_target="tpu_custom_call", output_to_operand_aliasing={{0}: (3, {}), {1}: (4, {})} | custom-call | flops 10223616 | bytes 5111808 | tf_op jit(solution)/shard_map/finish/pallas_call | solution.py:271
  82.5 3.0 %collective-permute-done.10.refs_1_ = f32[1,120,512]{2,1,0:T(8,128)S(1)} collective-permute-done((f32[1,120,512]{2,1,0:T(8,128)S(1)}, f32[1,120,512]{2,1,0:T(8,128)S(1)}, u32[]{:S(2)}, u32[]{:S(2)}) %collective-permute-start.10) | collective-permute-done | bytes 245792 | tf_op jit(solution)/shard_map/ppermute | solution.py:24
  85.5 1.0 %finish.5 = (f32[16,128,512]{2,1,0:T(8,128)}, f32[16,128,512]{2,1,0:T(8,128)}) custom-call(f32[1,120,512]{2,1,0:T(8,128)S(1)} %get-tuple-element.68.refs_0_, f32[1,120,512]{2,1,0:T(8,128)S(1)} %collective-permute-done.10.refs_1_, f32[16,128,512]{2,1,0:T(8,128)S(1)} %bitcast.10, ...), custom_call_target="tpu_custom_call", output_to_operand_aliasing={{0}: (3, {}), {1}: (4, {})} | custom-call | flops 2555904 | bytes 1277952 | tf_op jit(solution)/shard_map/finish/pallas_call | solution.py:271
  86.5 3.2 %collective-permute-done.11.refs_1_ = f32[1,120,512]{2,1,0:T(8,128)S(1)} collective-permute-done((f32[1,120,512]{2,1,0:T(8,128)S(1)}, f32[1,120,512]{2,1,0:T(8,128)S(1)}, u32[]{:S(2)}, u32[]{:S(2)}) %collective-permute-start.11) | collective-permute-done | bytes 245792 | tf_op jit(solution)/shard_map/ppermute | solution.py:24
  89.7 1.0 %finish_last.1 = (f32[16,128,512]{2,1,0:T(8,128)}, f32[16,128,512]{2,1,0:T(8,128)}) custom-call(f32[1,120,512]{2,1,0:T(8,128)S(1)} %get-tuple-element.74.refs_0_, f32[1,120,512]{2,1,0:T(8,128)S(1)} %collective-permute-done.11.refs_1_, f32[16,128,512]{2,1,0:T(8,128)S(1)} %bitcast.11, ...), custom_call_target="tpu_custom_call", output_to_operand_aliasing={{0}: (3, {}), {1}: (4, {})} | custom-call | tf_op jit(solution)/shard_map/finish_last/pallas_call | solution.py:271
Async XLA Ops:
  1.8 9.4 %collective-permute-start = (f32[1,120,512]{2,1,0:T(8,128)S(1)}, f32[1,120,512]{2,1,0:T(8,128)S(1)}, u32[]{:S(2)}, u32[]{:S(2)}) collective-permute-start(f32[1,120,512]{2,1,0:T(8,128)S(1)} %pair_x.1.refs_0_), channel_id=1, source_target_pairs={{0,16},{4,20},{8,24},{12,28},{16,0},{20,4},{24,8},{28,12},{1,17},{... | collective-permute-start | bytes 737288 | tf_op jit(solution)/shard_map/ppermute | solution.py:24
  8.1 30.0 %collective-permute-start.5 = (f32[5,120,512]{2,1,0:T(8,128)S(1)}, f32[5,120,512]{2,1,0:T(8,128)S(1)}, u32[]{:S(2)}, u32[]{:S(2)}) collective-permute-start(f32[5,120,512]{2,1,0:T(8,128)S(1)} %smooth_x.1.refs_0_), channel_id=1, source_target_pairs={{0,16},{4,20},{8,24},{12,28},{16,0},{20,4},{24,8},{28,12},{1,17},{... | collective-permute-start | bytes 3686408 | tf_op jit(solution)/shard_map/ppermute | solution.py:24
  12.8 11.3 %collective-permute-start.1 = (f32[2,64,512]{2,1,0:T(8,128)S(1)}, f32[2,64,512]{2,1,0:T(8,128)S(1)}, u32[]{:S(2)}, u32[]{:S(2)}) collective-permute-start(f32[2,64,512]{2,1,0:T(8,128)S(1)} %get-tuple-element.83), channel_id=1, source_target_pairs={{0,1},{1,2},{2,3},{3,0},{4,5},{5,6},{6,7},{7,4},{8,9},{9,10},{10,1... | collective-permute-start | bytes 786440 | tf_op jit(solution)/shard_map/ppermute | solution.py:24
  14.9 11.9 %collective-permute-start.2 = (f32[2,64,512]{2,1,0:T(8,128)S(1)}, f32[2,64,512]{2,1,0:T(8,128)S(1)}, u32[]{:S(2)}, u32[]{:S(2)}) collective-permute-start(f32[2,64,512]{2,1,0:T(8,128)S(1)} %get-tuple-element.82), channel_id=1, source_target_pairs={{0,3},{1,0},{2,1},{3,2},{4,7},{5,4},{6,5},{7,6},{8,11},{9,8},{10,9... | collective-permute-start | bytes 786440 | tf_op jit(solution)/shard_map/ppermute | solution.py:24
  30.5 13.9 %collective-permute-start.3 = (f32[3,64,512]{2,1,0:T(8,128)S(1)}, f32[3,64,512]{2,1,0:T(8,128)S(1)}, u32[]{:S(2)}, u32[]{:S(2)}) collective-permute-start(f32[3,64,512]{2,1,0:T(8,128)S(1)} %get-tuple-element.81), channel_id=1, source_target_pairs={{0,1},{1,2},{2,3},{3,0},{4,5},{5,6},{6,7},{7,4},{8,9},{9,10},{10,1... | collective-permute-start | bytes 1179656 | tf_op jit(solution)/shard_map/ppermute | solution.py:24
  31.8 19.2 %collective-permute-start.4 = (f32[3,64,512]{2,1,0:T(8,128)S(1)}, f32[3,64,512]{2,1,0:T(8,128)S(1)}, u32[]{:S(2)}, u32[]{:S(2)}) collective-permute-start(f32[3,64,512]{2,1,0:T(8,128)S(1)} %get-tuple-element.80), channel_id=1, source_target_pairs={{0,3},{1,0},{2,1},{3,2},{4,7},{5,4},{6,5},{7,6},{8,11},{9,8},{10,9... | collective-permute-start | bytes 1179656 | tf_op jit(solution)/shard_map/ppermute | solution.py:24
  34.4 40.8 %collective-permute-start.8 = (f32[4,120,512]{2,1,0:T(8,128)S(1)}, f32[4,120,512]{2,1,0:T(8,128)S(1)}, u32[]{:S(2)}, u32[]{:S(2)}) collective-permute-start(f32[4,120,512]{2,1,0:T(8,128)S(1)} %smooth_yx.3.refs_0_), channel_id=1, source_target_pairs={{0,16},{4,20},{8,24},{12,28},{16,0},{20,4},{24,8},{28,12},{1,17},{... | collective-permute-start | bytes 2949128 | tf_op jit(solution)/shard_map/ppermute | solution.py:24
  53.5 19.5 %copy-start = (f32[8,256,512]{2,1,0:T(8,128)S(1)}, f32[8,256,512]{2,1,0:T(8,128)}, u32[]{:S(2)}) copy-start(f32[8,256,512]{2,1,0:T(8,128)} %c_ref.7) | copy-start | bytes 12582916
  53.5 26.7 %collective-permute-start.9 = (f32[4,120,512]{2,1,0:T(8,128)S(1)}, f32[4,120,512]{2,1,0:T(8,128)S(1)}, u32[]{:S(2)}, u32[]{:S(2)}) collective-permute-start(f32[4,120,512]{2,1,0:T(8,128)S(1)} %smooth_yx.5.refs_0_), channel_id=1, source_target_pairs={{0,16},{4,20},{8,24},{12,28},{16,0},{20,4},{24,8},{28,12},{1,17},{... | collective-permute-start | bytes 2949128 | tf_op jit(solution)/shard_map/ppermute | solution.py:24
  54.5 13.9 %collective-permute-start.6 = (f32[3,64,512]{2,1,0:T(8,128)S(1)}, f32[3,64,512]{2,1,0:T(8,128)S(1)}, u32[]{:S(2)}, u32[]{:S(2)}) collective-permute-start(f32[3,64,512]{2,1,0:T(8,128)S(1)} %get-tuple-element.85), channel_id=1, source_target_pairs={{0,1},{1,2},{2,3},{3,0},{4,5},{5,6},{6,7},{7,4},{8,9},{9,10},{10,1... | collective-permute-start | bytes 1179656 | tf_op jit(solution)/shard_map/ppermute | solution.py:24
  54.9 18.1 %collective-permute-start.7 = (f32[3,64,512]{2,1,0:T(8,128)S(1)}, f32[3,64,512]{2,1,0:T(8,128)S(1)}, u32[]{:S(2)}, u32[]{:S(2)}) collective-permute-start(f32[3,64,512]{2,1,0:T(8,128)S(1)} %get-tuple-element.84), channel_id=1, source_target_pairs={{0,3},{1,0},{2,1},{3,2},{4,7},{5,4},{6,5},{7,6},{8,11},{9,8},{10,9... | collective-permute-start | bytes 1179656 | tf_op jit(solution)/shard_map/ppermute | solution.py:24
  60.3 25.2 %collective-permute-start.10 = (f32[1,120,512]{2,1,0:T(8,128)S(1)}, f32[1,120,512]{2,1,0:T(8,128)S(1)}, u32[]{:S(2)}, u32[]{:S(2)}) collective-permute-start(f32[1,120,512]{2,1,0:T(8,128)S(1)} %get-tuple-element.68.refs_0_), channel_id=1, source_target_pairs={{0,16},{4,20},{8,24},{12,28},{16,0},{20,4},{24,8},{28,12},{1,17},{... | collective-permute-start | bytes 737288 | tf_op jit(solution)/shard_map/ppermute | solution.py:24
  68.4 21.3 %collective-permute-start.11 = (f32[1,120,512]{2,1,0:T(8,128)S(1)}, f32[1,120,512]{2,1,0:T(8,128)S(1)}, u32[]{:S(2)}, u32[]{:S(2)}) collective-permute-start(f32[1,120,512]{2,1,0:T(8,128)S(1)} %get-tuple-element.74.refs_0_), channel_id=1, source_target_pairs={{0,16},{4,20},{8,24},{12,28},{16,0},{20,4},{24,8},{28,12},{1,17},{... | collective-permute-start | bytes 737288 | tf_op jit(solution)/shard_map/ppermute | solution.py:24
where the time goes:
time: 91 us; the launch traced here: 90.7 us
  waiting for transfers between devices  45.8 us (50%)
  Pallas kernels  21.9 us (24%)
  starting transfers between devices  19.9 us (22%)
  local copies, waits for them, and re-layouts  2.35 us (3%)
    ppermute x12, waiting for transfers between devices, passed_along(): return lax.ppermute(x, axis, [(i, (i + by) % peers) for i in range(peers)])  45.8 us
    pallas_call x12, Pallas kernels, call(): pl.pallas_call(kernel, grid=(steps,) if steps else (), in_specs=in_specs,...  21.9 us
    ppermute x12, starting transfers between devices, passed_along(): return lax.ppermute(x, axis, [(i, (i + by) % peers) for i in range(peers)])  19.9 us
    slice x3, local copies, waits for them, and re-layouts, halo(): source[start:stop, :REACH]  2.34 us
  transfers between devices with their start and end apart: 12, of which 11 were waited for; matrix products, arithmetic and copies ran while one was open for 3% of the time, Pallas kernels for 22%

commit v1 on v0

--- a/solution.py
+++ b/solution.py
@@ -14,7 +14,7 @@
 STRIP = 8
 UNIT_ROWS = 128
 FIRST_PLANES = 3
-LATER_GROUPS = (((2, 1),), ((2, 1), (1, 2)))
+LATER_GROUPS = (((2, 0),), ((1, 0), (1, 1), (1, 2)))
 
 kernel_weights = (0.0625, 0.25, 0.375, 0.25, 0.0625)
 
@@ -174,13 +174,17 @@
     return groups
 
 
-def yx_kernel(before_ref, c_ref, after_ref, *refs):
-    *out_refs, matrix_ref, smooth_ref = refs
-    pl.when(pl.program_id(0) == 0)(lambda: fill_matrix(matrix_ref, x_taps()))
+def y_smoothed(before_ref, c_ref, after_ref, smooth_ref):
     for within in range(TAP_DILATION // STRIP):
         groups = y_sums(extended_groups(before_ref, c_ref, after_ref, within * STRIP))
         for group, strip in enumerate(groups):
             smooth_ref[pl.ds(group * TAP_DILATION + within * STRIP, STRIP), :] = strip * (1.0 / 16.0)
+
+
+def yx_kernel(before_ref, c_ref, after_ref, *refs):
+    *out_refs, matrix_ref, smooth_ref = refs
+    pl.when(pl.program_id(0) == 0)(lambda: fill_matrix(matrix_ref, x_taps()))
+    y_smoothed(before_ref, c_ref, after_ref, smooth_ref)
     places = [(ref, place) for ref in out_refs for place in range(ref.shape[0])]
     for unit, (ref, place) in enumerate(places):
         smooth = x_smoothed(smooth_ref[pl.ds(unit * UNIT_ROWS, UNIT_ROWS), :], matrix_ref[...])
@@ -194,6 +198,116 @@
         whole_ref[0, rows, :] = strip
 
     unpacked(weights, refs[: len(weights)], use)
+
+
+def group_of(shape):
+    return lane_of(shape) // TAP_DILATION
+
+
+def spread(tile, group):
+    tile = jnp.where(group_of(tile.shape) == group, tile, 0.0)
+    tile = tile + pltpu.roll(tile, 2 * TAP_DILATION, 1)
+    return tile + pltpu.roll(tile, TAP_DILATION, 1)
+
+
+def strip_rows(rows, ahead):
+    per_group = TAP_DILATION // STRIP
+    strip = lax.rem(lax.axis_index("gy") + ahead, per_group)
+    return pl.ds(pl.multiple_of(rows - TAP_DILATION + strip * STRIP, STRIP), STRIP)
+
+
+def short_strips(rows):
+    half = rows - UNIT_ROWS
+    fixed = [pl.ds(row, STRIP) for row in range(0, rows - TAP_DILATION, STRIP)]
+    moving = [strip_rows(rows, ahead) for ahead in range(1, TAP_DILATION // STRIP)]
+    return fixed[: half // STRIP], fixed[half // STRIP :] + moving
+
+
+def short_tiles(rows, width):
+    return (rows // STRIP - 3) * (width // LANES)
+
+
+def short_kernel(before_ref, c_ref, after_ref, out_ref, matrix_ref, smooth_ref):
+    plane = pl.program_id(0)
+
+    @pl.when(plane == 0)
+    def _():
+        fill_matrix(matrix_ref, x_taps())
+        out_ref[out_ref.shape[0] - 1] = jnp.zeros((STRIP, LANES), jnp.float32)
+
+    y_smoothed(before_ref, c_ref, after_ref, smooth_ref)
+    rows, width = smooth_ref.shape
+    for start in range(0, rows, UNIT_ROWS):
+        unit = pl.ds(start, UNIT_ROWS)
+        smooth_ref[unit, :] = x_smoothed(smooth_ref[unit, :], matrix_ref[...])
+    index = plane * short_tiles(rows, width)
+    groups = LANES // TAP_DILATION
+    for places in short_strips(rows):
+        *places, last_place = places
+        last = smooth_ref[last_place, :]
+        for piece, place in enumerate(places):
+            strip = smooth_ref[place, :]
+            tile = piece // groups * LANES
+            moved = last[:, tile : tile + LANES]
+            shift = (groups - 1 - piece) % groups * TAP_DILATION
+            if shift:
+                moved = pltpu.roll(moved, shift, 1)
+            for start in range(0, width - LANES, LANES):
+                out_ref[index] = strip[:, start : start + LANES]
+                index += 1
+            here = group_of(moved.shape) == groups - 1
+            out_ref[index] = jnp.where(here, moved, strip[:, width - LANES :])
+            index += 1
+    left = spread(last[:, width - LANES :], groups - 2)
+    end = out_ref.shape[0] - 1
+    out_ref[end] = jnp.where(group_of(left.shape) == plane, left, out_ref[end])
+
+
+def short_z_kernel(weights, *refs):
+    packed, (whole_ref, *sum_refs) = refs[: len(weights)], refs[-4:]
+    rows, width = whole_ref.shape[1:]
+    plane = pl.program_id(0)
+    index = plane * short_tiles(rows, width)
+    groups, tiles = LANES // TAP_DILATION, width // LANES
+    for places in short_strips(rows):
+        *places, last_place = places
+        last = [None] * tiles
+        for piece, place in enumerate(places):
+            strip = [weighted(weights, [ref[index + tile] for ref in packed]) for tile in range(tiles)]
+            index += tiles
+            tile, group = divmod(piece, groups)
+            shift = (group + 1 - groups) % groups * TAP_DILATION
+            moved = pltpu.roll(strip[-1], shift, 1) if shift else strip[-1]
+            here = group_of(moved.shape) == group
+            last[tile] = moved if last[tile] is None else jnp.where(here, moved, last[tile])
+            whole_ref[0, place, :] = completed(jnp.concatenate(strip, axis=1))
+        if len(places) < tiles * groups - 1:
+            end = packed[0].shape[0] - 1
+            left = spread(weighted(weights, [ref[end] for ref in packed]), plane)
+            last[-1] = jnp.where(group_of(left.shape) == groups - 2, left, last[-1])
+        whole_ref[0, last_place, :] = completed(jnp.concatenate(last, axis=1))
+
+    groups = rows // TAP_DILATION
+    for ahead in range(TAP_DILATION // STRIP):
+        total = None
+        for group in range(groups if ahead else groups - 1):
+            strip = whole_ref[0, strip_rows((group + 1) * TAP_DILATION, ahead), :]
+            if total is None:
+                total = strip
+            else:
+                total = total + strip if group % 2 == 0 else total - strip
+        if ahead:
+            sum_refs[ahead - 1][0] = total
+        else:
+            whole_ref[0, strip_rows(rows, 0), :] = total
+
+
+def short_finish_kernel(whole_ref, *refs):
+    *sum_refs, c_ref, _, _, detail_ref, coarse_ref = refs
+    missing = strip_rows(whole_ref.shape[1], 0)
+    coarse_ref[...] = whole_ref[...]
+    coarse_ref[0, missing, :] = whole_ref[0, missing, :] + sum(ref[0] for ref in sum_refs)
+    detail_ref[...] = c_ref[...] - coarse_ref[...]
 
 
 def pair_z_kernel(weights, *refs):
@@ -259,6 +373,10 @@
 
 def anywhere():
     return pl.BlockSpec(memory_space=pl.ANY)
+
+
+def tiles_of(pieces):
+    return pl.BlockSpec((pieces, STRIP, LANES), lambda step: (0, 0, 0))
 
 
 def in_vmem():
@@ -288,6 +406,11 @@
 
 def f32(*shape):
     return jax.ShapeDtypeStruct(shape, jnp.float32)
+
+
+def can_shorten(rows, width):
+    strips = TAP_DILATION // STRIP
+    return lax.axis_size("gy") == strips and rows // TAP_DILATION % 2 == 0 and UNIT_ROWS // STRIP == width // TAP_DILATION
 
 
 def shards(coarse_six):
@@ -349,27 +472,45 @@
         scratch=[matrix, pltpu.VMEM((UNIT_ROWS, width), jnp.float32)],
     )
 
-    later = []
+    later, short_sent = [], []
     start = FIRST_PLANES
     sums, ready = lax.optimization_barrier((sums, coarse_six))
     near = halo(ready, start, start + sum(size for size, _ in LATER_GROUPS[0]))
     for number, sizes in enumerate(LATER_GROUPS):
         offset = 0
         for size, messages in sizes:
-            depth = parts // messages
-            blocks = call(
-                yx_kernel,
-                "smooth_yx",
-                size,
-                [edge(offset), whole(start + offset), edge(offset)],
-                [packed(depth=depth)] * messages,
-                [f32(size * depth, short, width)] * messages,
-                [near[0], in_hbm(coarse_six), near[1]],
-                scratch=[matrix, pltpu.VMEM((rows, width), jnp.float32)],
-            )
-            for message, block in enumerate(blocks):
-                place = (start + offset) * parts + message * depth
-                later.append((place, size * depth, (block, *along_gz(block))))
+            place = start + offset
+            sources = [near[0], in_hbm(coarse_six), near[1]]
+            specs = [edge(offset), whole(place), edge(offset)]
+            scratch = [matrix, pltpu.VMEM((rows, width), jnp.float32)]
+            if messages or not can_shorten(rows, width):
+                messages = max(messages, 1)
+                depth = parts // messages
+                blocks = call(
+                    yx_kernel,
+                    "smooth_yx",
+                    size,
+                    specs,
+                    [packed(depth=depth)] * messages,
+                    [f32(size * depth, short, width)] * messages,
+                    sources,
+                    scratch=scratch,
+                )
+                for message, block in enumerate(blocks):
+                    later.append((place * parts + message * depth, size * depth, (block, *along_gz(block))))
+            else:
+                pieces = size * short_tiles(rows, width) + 1
+                block = call(
+                    short_kernel,
+                    "smooth_yx_short",
+                    size,
+                    specs,
+                    [tiles_of(pieces)],
+                    [f32(pieces, STRIP, LANES)],
+                    sources,
+                    scratch=scratch,
+                )[0]
+                short_sent.append((place, size, (block, *along_gz(block))))
             offset += size
         start += offset
         if number == 0:
@@ -391,6 +532,24 @@
             near = halo(ready, start, start + sum(size for size, _ in LATER_GROUPS[number + 1]))
             near, along_z = lax.optimization_barrier((near, along_z))
 
+    short_sums, shortened = [], sum(size for _, size, _ in short_sent)
+    if short_sent:
+        step = 0
+        for place, size, blocks in short_sent:
+            short_sums = call(
+                functools.partial(short_z_kernel, weights),
+                "smooth_z_short",
+                size,
+                [tiles_of(blocks[0].shape[0])] * count + [anywhere()] * len(short_sums),
+                [whole(step)] + [block_of(STRIP, width, step)] * 3,
+                [f32(shortened, rows, width)] + [f32(shortened, STRIP, width)] * 3,
+                [*blocks, *short_sums],
+                {count + at: at for at in range(len(short_sums))},
+            )
+            step += size
+        moved_sums = [passed_along(total, "gy", ahead) for ahead, total in enumerate(short_sums[1:], 1)]
+        block = short_sums[0]
+
     block, sides = lax.optimization_barrier((block, sides))
     outs = call(
         y_kernel,
@@ -401,6 +560,18 @@
         [f32(planes, rows, width)] * 2,
         [sides[0], along_z, sides[1], coarse_six],
     )
+    if short_sent:
+        outs, moved_sums = lax.optimization_barrier((outs, moved_sums))
+        outs = call(
+            short_finish_kernel,
+            "finish_short",
+            shortened,
+            [whole()] + [block_of(STRIP, width)] * 3 + [whole(short_sent[0][0])] + [anywhere()] * 2,
+            [whole(short_sent[0][0])] * 2,
+            [f32(planes, rows, width)] * 2,
+            [short_sums[0], *moved_sums, coarse_six, *outs],
+            {5: 0, 6: 1},
+        )
     outs = [out.reshape(units.shape) for out in outs]
     for place, size, blocks in later[:-1]:
         outs, blocks = lax.optimization_barrier((outs, blocks))

time: 91 us -> 90.2 us (level)
  waiting for transfers between devices: 45.8 us -> 37.8 us
  starting transfers between devices: 19.9 us -> 25.9 us
  Pallas kernels: 21.9 us -> 23.2 us
    ppermute x12 -> x16, waiting for transfers between devices: 45.8 us -> 37.8 us  [passed_along(): return lax.ppermute(x, axis, [(i, (i + by) % peers) for i in range(peers)])]
    ppermute x12 -> x16, starting transfers between devices: 19.9 us -> 25.9 us  [passed_along(): return lax.ppermute(x, axis, [(i, (i + by) % peers) for i in range(peers)])]
    pallas_call x12 -> x15, Pallas kernels: 21.9 us -> 23.2 us  [call(): pl.pallas_call(kernel, grid=(steps,) if steps else (), in_specs=in_specs,...]
  transfers between devices with their start and end apart: 12 -> 16, of which waited for: 11 -> 11; matrix products, arithmetic and copies ran while one was open for 3% -> 3% of each run, Pallas kernels for 22% -> 23%
where the time goes in v1:
time: 90.2 us; the launch traced here: 89.9 us
  waiting for transfers between devices  37.8 us (42%)
  starting transfers between devices  25.9 us (29%)
  Pallas kernels  23.2 us (26%)
  local copies, waits for them, and re-layouts  2.33 us (3%)
    ppermute x16, waiting for transfers between devices, passed_along(): return lax.ppermute(x, axis, [(i, (i + by) % peers) for i in range(peers)])  37.8 us
    ppermute x16, starting transfers between devices, passed_along(): return lax.ppermute(x, axis, [(i, (i + by) % peers) for i in range(peers)])  25.9 us
    pallas_call x15, Pallas kernels, call(): pl.pallas_call(kernel, grid=(steps,) if steps else (), in_specs=in_specs,...  23.2 us
    slice x3, local copies, waits for them, and re-layouts, halo(): source[start:stop, :REACH]  2.33 us
  transfers between devices with their start and end apart: 16, of which 11 were waited for; matrix products, arithmetic and copies ran while one was open for 3% of the time, Pallas kernels for 23%

profile of v1, /device:TPU:0, one launch (start us, length us, event | category | flops | bytes accessed | tf_op | source)
XLA Modules:
  0.0 89.9 jit_solution(466447175914447125)
XLA Ops:
  0.6 1.1 %pair_x.1.refs_0_ = f32[1,120,512]{2,1,0:T(8,128)S(1)} custom-call(f32[16,128,512]{2,1,0:T(8,128)} %bitcast.6), custom_call_target="tpu_custom_call" | custom-call | tf_op jit(solution)/shard_map/pair_x/pallas_call | solution.py:389
  1.8 3.0 %collective-permute-start = (f32[1,120,512]{2,1,0:T(8,128)S(1)}, f32[1,120,512]{2,1,0:T(8,128)S(1)}, u32[]{:S(2)}, u32[]{:S(2)}) collective-permute-start(f32[1,120,512]{2,1,0:T(8,128)S(1)} %pair_x.1.refs_0_), channel_id=1, source_target_pairs={{0,16},{4,20},{8,24},{12,28},{16,0},{20,4},{24,8},{28,12},{1,17},{... | collective-permute-start | bytes 737288 | tf_op jit(solution)/shard_map/ppermute | solution.py:24
  4.8 3.3 %smooth_x.1.refs_0_ = f32[5,120,512]{2,1,0:T(8,128)S(1)} custom-call(f32[16,128,512]{2,1,0:T(8,128)} %bitcast.7), custom_call_target="tpu_custom_call" | custom-call | tf_op jit(solution)/shard_map/smooth_x/pallas_call | solution.py:389
  8.1 0.1 collective-permute-start.5
  8.2 3.0 %collective-permute-done.refs_1_ = f32[1,120,512]{2,1,0:T(8,128)S(1)} collective-permute-done((f32[1,120,512]{2,1,0:T(8,128)S(1)}, f32[1,120,512]{2,1,0:T(8,128)S(1)}, u32[]{:S(2)}, u32[]{:S(2)}) %collective-permute-start) | collective-permute-done | bytes 245792 | tf_op jit(solution)/shard_map/ppermute | solution.py:24
  11.1 0.6 smooth_zx.1.refs_2_
  11.7 1.1 %fusion.1 = (f32[2,64,512]{2,1,0:T(8,128)S(1)}, f32[2,64,512]{2,1,0:T(8,128)S(1)}) fusion(f32[8,256,512]{2,1,0:T(8,128)} %c_ref.9), kind=kLoop, calls=%fused_computation.1 | loop fusion | bytes 1048576 | tf_op jit(solution)/shard_map/slice | solution.py:431
  12.8 2.1 %collective-permute-start.1 = (f32[2,64,512]{2,1,0:T(8,128)S(1)}, f32[2,64,512]{2,1,0:T(8,128)S(1)}, u32[]{:S(2)}, u32[]{:S(2)}) collective-permute-start(f32[2,64,512]{2,1,0:T(8,128)S(1)} %get-tuple-element.101), channel_id=1, source_target_pairs={{0,1},{1,2},{2,3},{3,0},{4,5},{5,6},{6,7},{7,4},{8,9},{9,10},{10,1... | collective-permute-start | bytes 786440 | tf_op jit(solution)/shard_map/ppermute | solution.py:24
  14.9 2.1 %collective-permute-start.2 = (f32[2,64,512]{2,1,0:T(8,128)S(1)}, f32[2,64,512]{2,1,0:T(8,128)S(1)}, u32[]{:S(2)}, u32[]{:S(2)}) collective-permute-start(f32[2,64,512]{2,1,0:T(8,128)S(1)} %get-tuple-element.100), channel_id=1, source_target_pairs={{0,3},{1,0},{2,1},{3,2},{4,7},{5,4},{6,5},{7,6},{8,11},{9,8},{10,9... | collective-permute-start | bytes 786440 | tf_op jit(solution)/shard_map/ppermute | solution.py:24
  16.9 7.2 %collective-permute-done.1.before_ref = f32[2,64,512]{2,1,0:T(8,128)S(1)} collective-permute-done((f32[2,64,512]{2,1,0:T(8,128)S(1)}, f32[2,64,512]{2,1,0:T(8,128)S(1)}, u32[]{:S(2)}, u32[]{:S(2)}) %collective-permute-start.1) | collective-permute-done | bytes 262176 | tf_op jit(solution)/shard_map/ppermute | solution.py:24
  24.1 2.6 %collective-permute-done.2.after_ref = f32[2,64,512]{2,1,0:T(8,128)S(1)} collective-permute-done((f32[2,64,512]{2,1,0:T(8,128)S(1)}, f32[2,64,512]{2,1,0:T(8,128)S(1)}, u32[]{:S(2)}, u32[]{:S(2)}) %collective-permute-start.2) | collective-permute-done | bytes 262176 | tf_op jit(solution)/shard_map/ppermute | solution.py:24
  26.7 2.7 %smooth_yx_short.2.refs_0_ = f32[233,8,128]{2,1,0:T(8,128)S(1)} custom-call(f32[2,64,512]{2,1,0:T(8,128)S(1)} %collective-permute-done.1.before_ref, f32[8,256,512]{2,1,0:T(8,128)} %c_ref.9, f32[2,64,512]{2,1,0:T(8,128)S(1)} %collective-permute-done.2.after_ref), custom_call_target="tpu_custom_call" | custom-call | flops 6963200 | bytes 3481600 | tf_op jit(solution)/shard_map/smooth_yx_short/pallas_call | solution.py:389
  29.5 1.6 %collective-permute-start.7 = (f32[233,8,128]{2,1,0:T(8,128)S(1)}, f32[233,8,128]{2,1,0:T(8,128)S(1)}, u32[]{:S(2)}, u32[]{:S(2)}) collective-permute-start(f32[233,8,128]{2,1,0:T(8,128)S(1)} %smooth_yx_short.2.refs_0_), channel_id=1, source_target_pairs={{0,16},{4,20},{8,24},{12,28},{16,0},{20,4},{24,8},{28,12},{1,17},{... | collective-permute-start | bytes 2863112 | tf_op jit(solution)/shard_map/ppermute | solution.py:24
  31.1 1.2 %fusion = (f32[3,64,512]{2,1,0:T(8,128)S(1)}, f32[3,64,512]{2,1,0:T(8,128)S(1)}) fusion(f32[8,256,512]{2,1,0:T(8,128)} %c_ref.9), kind=kLoop, calls=%fused_computation | loop fusion | bytes 1572864 | tf_op jit(solution)/shard_map/slice | solution.py:431
  32.2 1.2 %collective-permute-start.3 = (f32[3,64,512]{2,1,0:T(8,128)S(1)}, f32[3,64,512]{2,1,0:T(8,128)S(1)}, u32[]{:S(2)}, u32[]{:S(2)}) collective-permute-start(f32[3,64,512]{2,1,0:T(8,128)S(1)} %get-tuple-element.99), channel_id=1, source_target_pairs={{0,1},{1,2},{2,3},{3,0},{4,5},{5,6},{6,7},{7,4},{8,9},{9,10},{10,1... | collective-permute-start | bytes 1179656 | tf_op jit(solution)/shard_map/ppermute | solution.py:24
  33.4 2.7 %collective-permute-start.4 = (f32[3,64,512]{2,1,0:T(8,128)S(1)}, f32[3,64,512]{2,1,0:T(8,128)S(1)}, u32[]{:S(2)}, u32[]{:S(2)}) collective-permute-start(f32[3,64,512]{2,1,0:T(8,128)S(1)} %get-tuple-element.98), channel_id=1, source_target_pairs={{0,3},{1,0},{2,1},{3,2},{4,7},{5,4},{6,5},{7,6},{8,11},{9,8},{10,9... | collective-permute-start | bytes 1179656 | tf_op jit(solution)/shard_map/ppermute | solution.py:24
  36.1 2.0 %collective-permute-done.5.refs_1_ = f32[5,120,512]{2,1,0:T(8,128)S(1)} collective-permute-done((f32[5,120,512]{2,1,0:T(8,128)S(1)}, f32[5,120,512]{2,1,0:T(8,128)S(1)}, u32[]{:S(2)}, u32[]{:S(2)}) %collective-permute-start.5) | collective-permute-done | bytes 1228832 | tf_op jit(solution)/shard_map/ppermute | solution.py:24
  38.1 1.1 %smooth_z.1 = f32[6,128,512]{2,1,0:T(8,128)S(1)} custom-call(f32[5,120,512]{2,1,0:T(8,128)S(1)} %smooth_x.1.refs_0_, f32[5,120,512]{2,1,0:T(8,128)S(1)} %collective-permute-done.5.refs_1_, f32[6,128,512]{2,1,0:T(8,128)S(1)} %smooth_zx.1.refs_2_), custom_call_target="tpu_custom_call", output_to_operand_aliasing={{}: (2, {})} | custom-call | flops 7536640 | bytes 3768320 | tf_op jit(solution)/shard_map/smooth_z/pallas_call | solution.py:389
  39.3 6.9 %collective-permute-done.3.before_ref = f32[3,64,512]{2,1,0:T(8,128)S(1)} collective-permute-done((f32[3,64,512]{2,1,0:T(8,128)S(1)}, f32[3,64,512]{2,1,0:T(8,128)S(1)}, u32[]{:S(2)}, u32[]{:S(2)}) %collective-permute-start.3) | collective-permute-done | bytes 393248 | tf_op jit(solution)/shard_map/ppermute | solution.py:24
  46.2 5.5 %collective-permute-done.4.after_ref = f32[3,64,512]{2,1,0:T(8,128)S(1)} collective-permute-done((f32[3,64,512]{2,1,0:T(8,128)S(1)}, f32[3,64,512]{2,1,0:T(8,128)S(1)}, u32[]{:S(2)}, u32[]{:S(2)}) %collective-permute-start.4) | collective-permute-done | bytes 393248 | tf_op jit(solution)/shard_map/ppermute | solution.py:24
  51.7 2.0 %smooth_yx_short.3.refs_0_ = f32[117,8,128]{2,1,0:T(8,128)S(1)} custom-call(f32[3,64,512]{2,1,0:T(8,128)S(1)} %collective-permute-done.3.before_ref, f32[8,256,512]{2,1,0:T(8,128)} %c_ref.9, f32[3,64,512]{2,1,0:T(8,128)S(1)} %collective-permute-done.4.after_ref), custom_call_target="tpu_custom_call" | custom-call | flops 2531328 | bytes 1265664 | tf_op jit(solution)/shard_map/smooth_yx_short/pallas_call | solution.py:389
  53.6 1.2 %collective-permute-start.6 = (f32[117,8,128]{2,1,0:T(8,128)S(1)}, f32[117,8,128]{2,1,0:T(8,128)S(1)}, u32[]{:S(2)}, u32[]{:S(2)}) collective-permute-start(f32[117,8,128]{2,1,0:T(8,128)S(1)} %smooth_yx_short.3.refs_0_), channel_id=1, source_target_pairs={{0,16},{4,20},{8,24},{12,28},{16,0},{20,4},{24,8},{28,12},{1,17},{... | collective-permute-start | bytes 1437704 | tf_op jit(solution)/shard_map/ppermute | solution.py:24
  54.8 0.1 fusion.2
  54.9 0.4 collective-permute-start.8
  55.3 1.9 %smooth_yx.2.refs_0_ = f32[2,120,512]{2,1,0:T(8,128)S(1)} custom-call(f32[3,64,512]{2,1,0:T(8,128)S(1)} %collective-permute-done.3.before_ref, f32[8,256,512]{2,1,0:T(8,128)} %c_ref.9, f32[3,64,512]{2,1,0:T(8,128)S(1)} %collective-permute-done.4.after_ref), custom_call_target="tpu_custom_call" | custom-call | flops 2555904 | bytes 1277952 | tf_op jit(solution)/shard_map/smooth_yx/pallas_call | solution.py:389
  57.2 0.9 collective-permute-start.13
  58.1 0.0 copy-start
  58.1 3.5 %collective-permute-start.9 = (f32[3,64,512]{2,1,0:T(8,128)S(1)}, f32[3,64,512]{2,1,0:T(8,128)S(1)}, u32[]{:S(2)}, u32[]{:S(2)}) collective-permute-start(f32[3,64,512]{2,1,0:T(8,128)S(1)} %get-tuple-element.102), channel_id=1, source_target_pairs={{0,3},{1,0},{2,1},{3,2},{4,7},{5,4},{6,5},{7,6},{8,11},{9,8},{10,9... | collective-permute-start | bytes 1179656 | tf_op jit(solution)/shard_map/ppermute | solution.py:24
  61.6 1.9 %smooth_yx.3 = (f32[1,120,512]{2,1,0:T(8,128)S(1)}, f32[1,120,512]{2,1,0:T(8,128)S(1)}) custom-call(f32[3,64,512]{2,1,0:T(8,128)S(1)} %collective-permute-done.3.before_ref, f32[8,256,512]{2,1,0:T(8,128)} %c_ref.9, f32[3,64,512]{2,1,0:T(8,128)S(1)} %collective-permute-done.4.after_ref), custom_call_target="tpu_custom_call" | custom-call | flops 2555904 | bytes 1277952 | tf_op jit(solution)/shard_map/smooth_yx/pallas_call | solution.py:389
  63.5 0.0 collective-permute-done.7.refs_1_
  63.5 1.3 %collective-permute-start.14 = (f32[1,120,512]{2,1,0:T(8,128)S(1)}, f32[1,120,512]{2,1,0:T(8,128)S(1)}, u32[]{:S(2)}, u32[]{:S(2)}) collective-permute-start(f32[1,120,512]{2,1,0:T(8,128)S(1)} %get-tuple-element.85.refs_0_), channel_id=1, source_target_pairs={{0,16},{4,20},{8,24},{12,28},{16,0},{20,4},{24,8},{28,12},{1,17},{... | collective-permute-start | bytes 737288 | tf_op jit(solution)/shard_map/ppermute | solution.py:24
  64.8 4.0 %collective-permute-done.6.refs_1_ = f32[117,8,128]{2,1,0:T(8,128)S(1)} collective-permute-done((f32[117,8,128]{2,1,0:T(8,128)S(1)}, f32[117,8,128]{2,1,0:T(8,128)S(1)}, u32[]{:S(2)}, u32[]{:S(2)}) %collective-permute-start.6) | collective-permute-done | bytes 479264 | tf_op jit(solution)/shard_map/ppermute | solution.py:24
  68.8 1.9 %collective-permute-start.15 = (f32[1,120,512]{2,1,0:T(8,128)S(1)}, f32[1,120,512]{2,1,0:T(8,128)S(1)}, u32[]{:S(2)}, u32[]{:S(2)}) collective-permute-start(f32[1,120,512]{2,1,0:T(8,128)S(1)} %get-tuple-element.92.refs_0_), channel_id=1, source_target_pairs={{0,16},{4,20},{8,24},{12,28},{16,0},{20,4},{24,8},{28,12},{1,17},{... | collective-permute-start | bytes 737288 | tf_op jit(solution)/shard_map/ppermute | solution.py:24
  70.7 0.7 smooth_z_short.2
  71.4 0.3 smooth_z_short.3
  71.7 0.0 collective-permute-done.8.before_ref
  71.7 1.6 %collective-permute-start.10 = (f32[3,8,512]{2,1,0:T(8,128)S(1)}, f32[3,8,512]{2,1,0:T(8,128)S(1)}, u32[]{:S(2)}, u32[]{:S(2)}) collective-permute-start(f32[3,8,512]{2,1,0:T(8,128)S(1)} %get-tuple-element.68), channel_id=1, source_target_pairs={{0,1},{1,2},{2,3},{3,0},{4,5},{5,6},{6,7},{7,4},{8,9},{9,10},{10,1... | collective-permute-start | bytes 147464 | tf_op jit(solution)/shard_map/ppermute | solution.py:24
  73.3 2.8 %collective-permute-done.9.after_ref = f32[3,64,512]{2,1,0:T(8,128)S(1)} collective-permute-done((f32[3,64,512]{2,1,0:T(8,128)S(1)}, f32[3,64,512]{2,1,0:T(8,128)S(1)}, u32[]{:S(2)}, u32[]{:S(2)}) %collective-permute-start.9) | collective-permute-done | bytes 393248 | tf_op jit(solution)/shard_map/ppermute | solution.py:24
  76.2 0.6 collective-permute-start.11
  76.8 0.9 collective-permute-done.10.refs_0_
  77.6 1.8 %collective-permute-start.12 = (f32[3,8,512]{2,1,0:T(8,128)S(1)}, f32[3,8,512]{2,1,0:T(8,128)S(1)}, u32[]{:S(2)}, u32[]{:S(2)}) collective-permute-start(f32[3,8,512]{2,1,0:T(8,128)S(1)} %get-tuple-element.70), channel_id=1, source_target_pairs={{0,3},{1,0},{2,1},{3,2},{4,7},{5,4},{6,5},{7,6},{8,11},{9,8},{10,9... | collective-permute-start | bytes 147464 | tf_op jit(solution)/shard_map/ppermute | solution.py:24
  79.4 0.0 copy-done
  79.4 2.2 %smooth_y.1 = (f32[8,256,512]{2,1,0:T(8,128)}, f32[8,256,512]{2,1,0:T(8,128)}) custom-call(f32[3,64,512]{2,1,0:T(8,128)S(1)} %collective-permute-done.8.before_ref, f32[3,256,512]{2,1,0:T(8,128)S(1)} %bitcast.12, f32[3,64,512]{2,1,0:T(8,128)S(1)} %collective-permute-done.9.after_ref, f32[8,256,512]{2,1,0:T(8,128)S(1)} %copy-done), custom_call_target="tpu_custom_call" | custom-call | flops 14155776 | bytes 7077888 | tf_op jit(solution)/shard_map/smooth_y/pallas_call | solution.py:389
  81.6 0.6 collective-permute-done.11.refs_1_
  82.2 0.0 collective-permute-done.12.refs_2_
  82.2 2.1 %finish_short.1 = (f32[8,256,512]{2,1,0:T(8,128)}, f32[8,256,512]{2,1,0:T(8,128)}) custom-call(f32[3,256,512]{2,1,0:T(8,128)S(1)} %get-tuple-element.62.whole_ref, f32[3,8,512]{2,1,0:T(8,128)S(1)} %collective-permute-done.10.refs_0_, f32[3,8,512]{2,1,0:T(8,128)S(1)} %collective-permute-done.11.refs_1_, ...), custom_call_target="tpu_custom_call", output_to_operand_aliasing={{0}: (5, {}), {1}: (6, {})} | custom-call | flops 12877824 | bytes 6438912 | tf_op jit(solution)/shard_map/finish_short/pallas_call | solution.py:389
  84.3 0.0 collective-permute-done.13.refs_1_
  84.3 1.3 %finish.2 = (f32[16,128,512]{2,1,0:T(8,128)}, f32[16,128,512]{2,1,0:T(8,128)}) custom-call(f32[2,120,512]{2,1,0:T(8,128)S(1)} %smooth_yx.2.refs_0_, f32[2,120,512]{2,1,0:T(8,128)S(1)} %collective-permute-done.13.refs_1_, f32[16,128,512]{2,1,0:T(8,128)S(1)} %bitcast.8, f32[16,128,512]{2,1,0:T(8,128)} %bitcast.13, ...), custom_call_target="tpu_custom_call", output_to_operand_aliasing={{0}: (3, {}), {1}: (4, {})} | custom-call | flops 5111808 | bytes 2555904 | tf_op jit(solution)/shard_map/finish/pallas_call | solution.py:389
  85.6 0.0 collective-permute-done.14.refs_1_
  85.6 1.0 %finish.3 = (f32[16,128,512]{2,1,0:T(8,128)}, f32[16,128,512]{2,1,0:T(8,128)}) custom-call(f32[1,120,512]{2,1,0:T(8,128)S(1)} %get-tuple-element.85.refs_0_, f32[1,120,512]{2,1,0:T(8,128)S(1)} %collective-permute-done.14.refs_1_, f32[16,128,512]{2,1,0:T(8,128)S(1)} %bitcast.9, ...), custom_call_target="tpu_custom_call", output_to_operand_aliasing={{0}: (3, {}), {1}: (4, {})} | custom-call | flops 2555904 | bytes 1277952 | tf_op jit(solution)/shard_map/finish/pallas_call | solution.py:389
  86.6 2.2 %collective-permute-done.15.refs_1_ = f32[1,120,512]{2,1,0:T(8,128)S(1)} collective-permute-done((f32[1,120,512]{2,1,0:T(8,128)S(1)}, f32[1,120,512]{2,1,0:T(8,128)S(1)}, u32[]{:S(2)}, u32[]{:S(2)}) %collective-permute-start.15) | collective-permute-done | bytes 245792 | tf_op jit(solution)/shard_map/ppermute | solution.py:24
  88.9 1.0 %finish_last.1 = (f32[16,128,512]{2,1,0:T(8,128)}, f32[16,128,512]{2,1,0:T(8,128)}) custom-call(f32[1,120,512]{2,1,0:T(8,128)S(1)} %get-tuple-element.92.refs_0_, f32[1,120,512]{2,1,0:T(8,128)S(1)} %collective-permute-done.15.refs_1_, f32[16,128,512]{2,1,0:T(8,128)S(1)} %bitcast.10, ...), custom_call_target="tpu_custom_call", output_to_operand_aliasing={{0}: (3, {}), {1}: (4, {})} | custom-call | tf_op jit(solution)/shard_map/finish_last/pallas_call | solution.py:389
Async XLA Ops:
  1.8 9.4 %collective-permute-start = (f32[1,120,512]{2,1,0:T(8,128)S(1)}, f32[1,120,512]{2,1,0:T(8,128)S(1)}, u32[]{:S(2)}, u32[]{:S(2)}) collective-permute-start(f32[1,120,512]{2,1,0:T(8,128)S(1)} %pair_x.1.refs_0_), channel_id=1, source_target_pairs={{0,16},{4,20},{8,24},{12,28},{16,0},{20,4},{24,8},{28,12},{1,17},{... | collective-permute-start | bytes 737288 | tf_op jit(solution)/shard_map/ppermute | solution.py:24
  8.1 30.0 %collective-permute-start.5 = (f32[5,120,512]{2,1,0:T(8,128)S(1)}, f32[5,120,512]{2,1,0:T(8,128)S(1)}, u32[]{:S(2)}, u32[]{:S(2)}) collective-permute-start(f32[5,120,512]{2,1,0:T(8,128)S(1)} %smooth_x.1.refs_0_), channel_id=1, source_target_pairs={{0,16},{4,20},{8,24},{12,28},{16,0},{20,4},{24,8},{28,12},{1,17},{... | collective-permute-start | bytes 3686408 | tf_op jit(solution)/shard_map/ppermute | solution.py:24
  12.8 11.3 %collective-permute-start.1 = (f32[2,64,512]{2,1,0:T(8,128)S(1)}, f32[2,64,512]{2,1,0:T(8,128)S(1)}, u32[]{:S(2)}, u32[]{:S(2)}) collective-permute-start(f32[2,64,512]{2,1,0:T(8,128)S(1)} %get-tuple-element.101), channel_id=1, source_target_pairs={{0,1},{1,2},{2,3},{3,0},{4,5},{5,6},{6,7},{7,4},{8,9},{9,10},{10,1... | collective-permute-start | bytes 786440 | tf_op jit(solution)/shard_map/ppermute | solution.py:24
  14.9 11.9 %collective-permute-start.2 = (f32[2,64,512]{2,1,0:T(8,128)S(1)}, f32[2,64,512]{2,1,0:T(8,128)S(1)}, u32[]{:S(2)}, u32[]{:S(2)}) collective-permute-start(f32[2,64,512]{2,1,0:T(8,128)S(1)} %get-tuple-element.100), channel_id=1, source_target_pairs={{0,3},{1,0},{2,1},{3,2},{4,7},{5,4},{6,5},{7,6},{8,11},{9,8},{10,9... | collective-permute-start | bytes 786440 | tf_op jit(solution)/shard_map/ppermute | solution.py:24
  29.5 34.0 %collective-permute-start.7 = (f32[233,8,128]{2,1,0:T(8,128)S(1)}, f32[233,8,128]{2,1,0:T(8,128)S(1)}, u32[]{:S(2)}, u32[]{:S(2)}) collective-permute-start(f32[233,8,128]{2,1,0:T(8,128)S(1)} %smooth_yx_short.2.refs_0_), channel_id=1, source_target_pairs={{0,16},{4,20},{8,24},{12,28},{16,0},{20,4},{24,8},{28,12},{1,17},{... | collective-permute-start | bytes 2863112 | tf_op jit(solution)/shard_map/ppermute | solution.py:24
  32.2 13.9 %collective-permute-start.3 = (f32[3,64,512]{2,1,0:T(8,128)S(1)}, f32[3,64,512]{2,1,0:T(8,128)S(1)}, u32[]{:S(2)}, u32[]{:S(2)}) collective-permute-start(f32[3,64,512]{2,1,0:T(8,128)S(1)} %get-tuple-element.99), channel_id=1, source_target_pairs={{0,1},{1,2},{2,3},{3,0},{4,5},{5,6},{6,7},{7,4},{8,9},{9,10},{10,1... | collective-permute-start | bytes 1179656 | tf_op jit(solution)/shard_map/ppermute | solution.py:24
  33.4 18.2 %collective-permute-start.4 = (f32[3,64,512]{2,1,0:T(8,128)S(1)}, f32[3,64,512]{2,1,0:T(8,128)S(1)}, u32[]{:S(2)}, u32[]{:S(2)}) collective-permute-start(f32[3,64,512]{2,1,0:T(8,128)S(1)} %get-tuple-element.98), channel_id=1, source_target_pairs={{0,3},{1,0},{2,1},{3,2},{4,7},{5,4},{6,5},{7,6},{8,11},{9,8},{10,9... | collective-permute-start | bytes 1179656 | tf_op jit(solution)/shard_map/ppermute | solution.py:24
  53.6 15.2 %collective-permute-start.6 = (f32[117,8,128]{2,1,0:T(8,128)S(1)}, f32[117,8,128]{2,1,0:T(8,128)S(1)}, u32[]{:S(2)}, u32[]{:S(2)}) collective-permute-start(f32[117,8,128]{2,1,0:T(8,128)S(1)} %smooth_yx_short.3.refs_0_), channel_id=1, source_target_pairs={{0,16},{4,20},{8,24},{12,28},{16,0},{20,4},{24,8},{28,12},{1,17},{... | collective-permute-start | bytes 1437704 | tf_op jit(solution)/shard_map/ppermute | solution.py:24
  54.9 16.8 %collective-permute-start.8 = (f32[3,64,512]{2,1,0:T(8,128)S(1)}, f32[3,64,512]{2,1,0:T(8,128)S(1)}, u32[]{:S(2)}, u32[]{:S(2)}) collective-permute-start(f32[3,64,512]{2,1,0:T(8,128)S(1)} %get-tuple-element.103), channel_id=1, source_target_pairs={{0,1},{1,2},{2,3},{3,0},{4,5},{5,6},{6,7},{7,4},{8,9},{9,10},{10,1... | collective-permute-start | bytes 1179656 | tf_op jit(solution)/shard_map/ppermute | solution.py:24
  57.2 27.1 %collective-permute-start.13 = (f32[2,120,512]{2,1,0:T(8,128)S(1)}, f32[2,120,512]{2,1,0:T(8,128)S(1)}, u32[]{:S(2)}, u32[]{:S(2)}) collective-permute-start(f32[2,120,512]{2,1,0:T(8,128)S(1)} %smooth_yx.2.refs_0_), channel_id=1, source_target_pairs={{0,16},{4,20},{8,24},{12,28},{16,0},{20,4},{24,8},{28,12},{1,17},{... | collective-permute-start | bytes 1474568 | tf_op jit(solution)/shard_map/ppermute | solution.py:24
  58.1 21.3 %copy-start = (f32[8,256,512]{2,1,0:T(8,128)S(1)}, f32[8,256,512]{2,1,0:T(8,128)}, u32[]{:S(2)}) copy-start(f32[8,256,512]{2,1,0:T(8,128)} %c_ref.9) | copy-start | bytes 12582916
  58.1 18.0 %collective-permute-start.9 = (f32[3,64,512]{2,1,0:T(8,128)S(1)}, f32[3,64,512]{2,1,0:T(8,128)S(1)}, u32[]{:S(2)}, u32[]{:S(2)}) collective-permute-start(f32[3,64,512]{2,1,0:T(8,128)S(1)} %get-tuple-element.102), channel_id=1, source_target_pairs={{0,3},{1,0},{2,1},{3,2},{4,7},{5,4},{6,5},{7,6},{8,11},{9,8},{10,9... | collective-permute-start | bytes 1179656 | tf_op jit(solution)/shard_map/ppermute | solution.py:24
  63.5 22.1 %collective-permute-start.14 = (f32[1,120,512]{2,1,0:T(8,128)S(1)}, f32[1,120,512]{2,1,0:T(8,128)S(1)}, u32[]{:S(2)}, u32[]{:S(2)}) collective-permute-start(f32[1,120,512]{2,1,0:T(8,128)S(1)} %get-tuple-element.85.refs_0_), channel_id=1, source_target_pairs={{0,16},{4,20},{8,24},{12,28},{16,0},{20,4},{24,8},{28,12},{1,17},{... | collective-permute-start | bytes 737288 | tf_op jit(solution)/shard_map/ppermute | solution.py:24
  68.8 20.0 %collective-permute-start.15 = (f32[1,120,512]{2,1,0:T(8,128)S(1)}, f32[1,120,512]{2,1,0:T(8,128)S(1)}, u32[]{:S(2)}, u32[]{:S(2)}) collective-permute-start(f32[1,120,512]{2,1,0:T(8,128)S(1)} %get-tuple-element.92.refs_0_), channel_id=1, source_target_pairs={{0,16},{4,20},{8,24},{12,28},{16,0},{20,4},{24,8},{28,12},{1,17},{... | collective-permute-start | bytes 737288 | tf_op jit(solution)/shard_map/ppermute | solution.py:24
  71.7 5.9 %collective-permute-start.10 = (f32[3,8,512]{2,1,0:T(8,128)S(1)}, f32[3,8,512]{2,1,0:T(8,128)S(1)}, u32[]{:S(2)}, u32[]{:S(2)}) collective-permute-start(f32[3,8,512]{2,1,0:T(8,128)S(1)} %get-tuple-element.68), channel_id=1, source_target_pairs={{0,1},{1,2},{2,3},{3,0},{4,5},{5,6},{6,7},{7,4},{8,9},{9,10},{10,1... | collective-permute-start | bytes 147464 | tf_op jit(solution)/shard_map/ppermute | solution.py:24
  76.2 6.0 %collective-permute-start.11 = (f32[3,8,512]{2,1,0:T(8,128)S(1)}, f32[3,8,512]{2,1,0:T(8,128)S(1)}, u32[]{:S(2)}, u32[]{:S(2)}) collective-permute-start(f32[3,8,512]{2,1,0:T(8,128)S(1)} %get-tuple-element.69), channel_id=1, source_target_pairs={{0,2},{1,3},{2,0},{3,1},{4,6},{5,7},{6,4},{7,5},{8,10},{9,11},{10,... | collective-permute-start | bytes 147464 | tf_op jit(solution)/shard_map/ppermute | solution.py:24
  77.6 4.6 %collective-permute-start.12 = (f32[3,8,512]{2,1,0:T(8,128)S(1)}, f32[3,8,512]{2,1,0:T(8,128)S(1)}, u32[]{:S(2)}, u32[]{:S(2)}) collective-permute-start(f32[3,8,512]{2,1,0:T(8,128)S(1)} %get-tuple-element.70), channel_id=1, source_target_pairs={{0,3},{1,0},{2,1},{3,2},{4,7},{5,4},{6,5},{7,6},{8,11},{9,8},{10,9... | collective-permute-start | bytes 147464 | tf_op jit(solution)/shard_map/ppermute | solution.py:24
